TPU v7x, 32 devices: a whole 2x2x4 slice. The times are simulated.
32 devices in a mesh: dp: 8 (over y, x, core), tensor: 4 (over z).
Axes of the slice: x: 2, y: 2, z: 4, core: 2. Of those that a mesh axis runs over, the one named last changes fastest.
Arguments:
- inputs: bfloat16 [2048, 1024], P(('dp', 'tensor')), may hold values from -6 to 6
- first_gain: float32 [1024], replicated, may hold values from 0.1 to 1.9
- entry_projection_weight: bfloat16 [3, 1024, 1024], P(None, 'dp', 'tensor'), may hold values from -0.1875 to 0.1875
- conv_weight: float32 [3, 1024], replicated, may hold values from -3 to 3
- out_weight: bfloat16 [1024, 1024], P('tensor', 'dp'), may hold values from -0.1875 to 0.1875
- second_gain: float32 [1024], replicated, may hold values from 0.1 to 1.9
- gate_up_weight: bfloat16 [2, 1024, 4608], P(None, 'dp', 'tensor'), may hold values from -0.1875 to 0.1875
- down_weight: bfloat16 [4608, 1024], P('tensor', 'dp'), may hold values from -0.09375 to 0.09375
- cotangent: bfloat16 [2048, 1024], P(('dp', 'tensor')), may hold values from -6 to 6
- lengths: int32 [4], replicated, may hold values from 1 to 1024, 2048 in all
Outputs:
- output: bfloat16 [2048, 1024], P(('dp', 'tensor'))
- input_grad: float32 [2048, 1024], P(('dp', 'tensor'))
- first_gain_grad: float32 [1024], replicated
- in_weight_grad: float32 [3, 1024, 1024], P(None, 'dp', 'tensor')
- filter_weight_gradient: float32 [3, 1024], replicated
- out_weight_grad: float32 [1024, 1024], P('tensor', 'dp')
- second_gain_grad: float32 [1024], replicated
- gate_up_grad: float32 [2, 1024, 4608], P(None, 'dp', 'tensor')
- down_grad: float32 [4608, 1024], P('tensor', 'dp')
Inputs may be any that keep to these rules, and one draw needn't show every extreme that they name: lengths of the 4 sequences packed end to end in token order; they sum to 2048, and the longest is exactly 1024.
All inputs are finite; a program needn't handle non-finite values.
Results may differ from a plain program's by a relative error of at most 0.012.
Values may be sent and summed in bfloat16 or wider, within the bound.
A program may use at most 128 MiB of HBM per device.

v0:
```python
import jax
import jax.numpy as jnp
from jax import lax
from jax.sharding import PartitionSpec as P

EPS = 1e-05


def passed_along(block, axis, distance):
    devices = range(lax.axis_size(axis))
    route = [(i - distance, i) for i in devices if i - distance in devices]
    return lax.ppermute(block, axis, route)


def rms_norm(values, gain):
    return values * lax.rsqrt(jnp.mean(values * values, axis=-1, keepdims=True) + EPS) * gain


def rms_back(values, gain, grad_out):
    scale = lax.rsqrt(jnp.mean(values * values, axis=-1, keepdims=True) + EPS)
    normal = values * scale
    weighted = gain * grad_out
    grad_in = scale * (weighted - normal * jnp.mean(normal * weighted, axis=-1, keepdims=True))
    return (grad_in, jnp.sum(normal * grad_out, axis=0))


def times_trans(left, right):
    return lax.dot_general(
        left, right, (((1,), (1,)), ((), ())), preferred_element_type=jnp.float32
    )


def trans_times(left, right):
    return lax.dot_general(
        left, right, (((0,), (0,)), ((), ())), preferred_element_type=jnp.float32
    )


def shards(
    inputs,
    first_gain,
    entry_projection_weight,
    conv_weight,
    out_weight,
    second_gain,
    gate_up_weight,
    down_weight,
    cotangent,
    lengths,
):
    own_rows = inputs.shape[0]
    group_rows = own_rows * lax.axis_size("tensor")
    channels = entry_projection_weight.shape[2]
    column = lax.axis_index("tensor") * channels
    start = lax.axis_index("dp") * group_rows
    ends = jnp.cumsum(lengths)
    places = start - 2 + jnp.arange(group_rows + 4, dtype=jnp.int32)
    segment = jnp.sum((places[:, None] >= ends[None, :]).astype(jnp.int32), axis=1)
    first_all = jnp.logical_and(segment[2:] == segment[1:-1], places[2:] >= 1).astype(jnp.float32)[
        :, None
    ]
    second_all = jnp.logical_and(segment[2:] == segment[:-2], places[2:] >= 2).astype(jnp.float32)[
        :, None
    ]
    first_keep = first_all[:group_rows]
    second_keep = second_all[:group_rows]
    kernel = lax.dynamic_slice_in_dim(conv_weight, column, channels, 1)
    residual = inputs.astype(jnp.float32)
    normed = lax.all_gather(
        rms_norm(residual, first_gain).astype(jnp.bfloat16), "tensor", axis=0, tiled=True
    )
    in_full, out_full, gate_up_full, down_full = (
        lax.all_gather(entry_projection_weight, "dp", axis=1, tiled=True),
        lax.all_gather(out_weight, "dp", axis=1, tiled=True),
        lax.all_gather(gate_up_weight, "dp", axis=1, tiled=True),
        lax.all_gather(down_weight, "dp", axis=1, tiled=True),
    )
    projected = jnp.einsum("td,kdc->ktc", normed, in_full, preferred_element_type=jnp.float32)
    input_gate_value = projected[0]
    c_value = projected[1]
    v_value = projected[2]
    product = (input_gate_value * v_value).astype(jnp.bfloat16)
    before = passed_along(product[-2:], "dp", 1)
    extended = jnp.concatenate([before, product], axis=0).astype(jnp.float32)
    mixed = (
        kernel[2] * extended[2:]
        + kernel[1] * first_keep * extended[1:-1]
        + kernel[0] * second_keep * extended[:-2]
    )
    gated = (c_value * mixed).astype(jnp.bfloat16)
    mixer_part = jnp.dot(gated, out_full, preferred_element_type=jnp.float32)
    middle = residual + lax.psum_scatter(mixer_part, "tensor", scatter_dimension=0, tiled=True)
    hidden_in = lax.all_gather(
        rms_norm(middle, second_gain).astype(jnp.bfloat16), "tensor", axis=0, tiled=True
    )
    gate_up = jnp.einsum("td,kdf->ktf", hidden_in, gate_up_full, preferred_element_type=jnp.float32)
    gate_value = gate_up[0]
    up_value = gate_up[1]
    sigmoid = jax.nn.sigmoid(gate_value)
    swish = gate_value * sigmoid
    hidden = (swish * up_value).astype(jnp.bfloat16)
    ffn_part = jnp.dot(hidden, down_full, preferred_element_type=jnp.float32)
    output = (
        middle
        + lax.psum_scatter(
            ffn_part.astype(jnp.bfloat16), "tensor", scatter_dimension=0, tiled=True
        ).astype(jnp.float32)
    ).astype(jnp.bfloat16)
    in_full, out_full, gate_up_full, down_full = (
        lax.all_gather(entry_projection_weight, "dp", axis=1, tiled=True),
        lax.all_gather(out_weight, "dp", axis=1, tiled=True),
        lax.all_gather(gate_up_weight, "dp", axis=1, tiled=True),
        lax.all_gather(down_weight, "dp", axis=1, tiled=True),
    )
    grad_rows = lax.all_gather(cotangent, "tensor", axis=0, tiled=True)
    grad_hidden = times_trans(grad_rows, down_full)
    down_part = trans_times(hidden, grad_rows)
    grad_gate = (grad_hidden * up_value * sigmoid * (1.0 + gate_value * (1.0 - sigmoid))).astype(
        jnp.bfloat16
    )
    grad_up = (grad_hidden * swish).astype(jnp.bfloat16)
    gate_up_stack = jnp.stack([grad_gate, grad_up])
    gate_up_part = jnp.einsum(
        "td,ktf->kdf", hidden_in, gate_up_stack, preferred_element_type=jnp.float32
    )
    hidden_back = jnp.einsum(
        "ktf,kdf->td", gate_up_stack, gate_up_full, preferred_element_type=jnp.float32
    )
    grad_hin = lax.psum_scatter(hidden_back, "tensor", scatter_dimension=0, tiled=True)
    second_back, second_part = rms_back(middle, second_gain, grad_hin)
    grad_middle = cotangent.astype(jnp.float32) + second_back
    branch_rows = lax.all_gather(grad_middle.astype(jnp.bfloat16), "tensor", axis=0, tiled=True)
    grad_gated = times_trans(branch_rows, out_full)
    out_part = trans_times(gated, branch_rows)
    output_gate_gradient = (grad_gated * mixed).astype(jnp.bfloat16)
    grad_mixed = (grad_gated * c_value).astype(jnp.bfloat16)
    after = passed_along(grad_mixed[:2], "dp", -1)
    grad_ext = jnp.concatenate([grad_mixed, after], axis=0).astype(jnp.float32)
    mixed_wide = grad_ext[:-2]
    kernel_part = jnp.stack(
        [
            jnp.sum(second_keep * extended[:-2] * mixed_wide, axis=0),
            jnp.sum(first_keep * extended[1:-1] * mixed_wide, axis=0),
            jnp.sum(extended[2:] * mixed_wide, axis=0),
        ]
    )
    kernel_full = lax.dynamic_update_slice_in_dim(
        jnp.zeros(conv_weight.shape, jnp.float32), kernel_part, column, 1
    )
    elementwise_product_gradient = (
        kernel[2] * grad_ext[:-2]
        + kernel[1] * first_all[1:-1] * grad_ext[1:-1]
        + kernel[0] * second_all[2:] * grad_ext[2:]
    )
    input_gate_gradient = (elementwise_product_gradient * v_value).astype(jnp.bfloat16)
    value_branch_gradient = (elementwise_product_gradient * input_gate_value).astype(jnp.bfloat16)
    stacked_projection_outputs = jnp.stack(
        [input_gate_gradient, output_gate_gradient, value_branch_gradient]
    )
    in_part = jnp.einsum(
        "td,ktc->kdc", normed, stacked_projection_outputs, preferred_element_type=jnp.float32
    )
    normed_back = jnp.einsum(
        "ktc,kdc->td", stacked_projection_outputs, in_full, preferred_element_type=jnp.float32
    )
    grad_normed = lax.psum_scatter(
        normed_back.astype(jnp.bfloat16), "tensor", scatter_dimension=0, tiled=True
    ).astype(jnp.float32)
    first_back, first_part = rms_back(residual, first_gain, grad_normed)
    input_grad = grad_middle + first_back
    in_grad, out_grad, gate_up_grad, down_grad = (
        lax.psum_scatter(in_part, "dp", scatter_dimension=1, tiled=True),
        lax.psum_scatter(out_part, "dp", scatter_dimension=1, tiled=True),
        lax.psum_scatter(gate_up_part, "dp", scatter_dimension=1, tiled=True),
        lax.psum_scatter(down_part, "dp", scatter_dimension=1, tiled=True),
    )
    first_gain_grad, second_gain_grad, conv_grad = lax.psum(
        (first_part, second_part, kernel_full), ("dp", "tensor")
    )
    return (
        output,
        input_grad,
        first_gain_grad,
        in_grad,
        conv_grad,
        out_grad,
        second_gain_grad,
        gate_up_grad,
        down_grad,
    )


def solution(mesh):
    in_specs = (
        P(("dp", "tensor"), None),
        P(),
        P(None, "dp", "tensor"),
        P(),
        P("tensor", "dp"),
        P(),
        P(None, "dp", "tensor"),
        P("tensor", "dp"),
        P(("dp", "tensor"), None),
        P(),
    )
    out_specs = (
        P(("dp", "tensor"), None),
        P(("dp", "tensor"), None),
        P(),
        P(None, "dp", "tensor"),
        P(),
        P("tensor", "dp"),
        P(),
        P(None, "dp", "tensor"),
        P("tensor", "dp"),
    )
    return jax.shard_map(shards, mesh=mesh, in_specs=in_specs, out_specs=out_specs, check_vma=False)
```

profile of v0, /device:TPU:0, one launch (start us, length us, event | category | flops | bytes accessed | tf_op | source)
XLA Modules:
  0.0 489.5 jit_solution(4341568830876603250)
XLA Ops:
  7.2 0.7 all-gather.4.cloned.1.call-update
  8.0 0.8 reduce-window.8
  8.9 11.7 %all_gather.30 = bf16[256,1024]{1,0:T(8,128)(2,1)S(1)} all-gather(bf16[256,128]{1,0:T(8,128)(2,1)} %param.14), channel_id=1, replica_groups=mesh['dp'=8,'tensor'=4] {'dp'}, dimensions={1}, use_global_device_ids=true | all-gather | bytes 589824 | tf_op jit(solution)/shard_map/all_gather | solution.py:74
  20.6 1.1 fusion.18
  21.8 1.0 fusion.15
  22.8 16.4 %all_gather.28 = bf16[256,1024]{1,0:T(8,128)(2,1)S(1)} all-gather(bf16[64,1024]{1,0:T(8,128)(2,1)S(1)} %fusion.15), channel_id=1, replica_groups=mesh['dp'=8,'tensor'=4] {'tensor'}, dimensions={0}, use_global_device_ids=true | all-gather | bytes 655360 | tf_op jit(solution)/shard_map/all_gather | solution.py:69
  39.3 0.7 fusion.35
  39.9 2.0 convolution_bitcast_fusion.5
  42.0 1.3 collective-permute-start
  43.3 0.9 fusion.34
  44.2 0.9 multiply_convert_fusion.8
  45.1 1.3 fusion.37
  46.5 0.7 all-gather.6.cloned.1.call-update
  47.8 21.5 %all_gather.34 = bf16[256,1024]{1,0:T(8,128)(2,1)} all-gather(bf16[64,1024]{1,0:T(8,128)(2,1)S(1)} %copy-done.13), channel_id=1, replica_groups=mesh['dp'=8,'tensor'=4] {'tensor'}, dimensions={0}, use_global_device_ids=true | all-gather | bytes 655360 | tf_op jit(solution)/shard_map/all_gather | solution.py:115
  69.3 13.1 %reduce-scatter.9.cloned.1.call-done = f32[64,1024]{1,0:T(8,128)} async-done(((f32[256,1024]{1,0:T(8,128)}), f32[64,1024]{1,0:T(8,128)}) %reduce-scatter.9.cloned.1.call-update) | async-done | bytes 262160 | tf_op jit(solution)/shard_map/reduce_scatter | solution.py:92
  82.4 1.1 multiply_reduce_fusion.5
  83.6 16.7 %all_gather.31 = bf16[256,1024]{1,0:T(8,128)(2,1)} all-gather(bf16[64,1024]{1,0:T(8,128)(2,1)S(1)} %multiply_convert_fusion.7), channel_id=1, replica_groups=mesh['dp'=8,'tensor'=4] {'tensor'}, dimensions={0}, use_global_device_ids=true | all-gather | bytes 655360 | tf_op jit(solution)/shard_map/all_gather | solution.py:93
  100.3 22.1 %all-gather.6.cloned.1.call-done = bf16[2,1024,1152]{2,1,0:T(8,128)(2,1)} async-done(((bf16[2,128,1152]{2,1,0:T(8,128)(2,1)}), bf16[2,1024,1152]{2,1,0:T(8,128)(2,1)}) %all-gather.6.cloned.1.call-update) | async-done | bytes 4718608 | tf_op jit(solution)/shard_map/all_gather | solution.py:75
  122.4 3.9 convolution_bitcast_fusion.1
  126.2 27.4 %all-gather.8.cloned.1.call-done = bf16[1152,1024]{1,0:T(8,128)(2,1)} async-done(((bf16[1152,128]{1,0:T(8,128)(2,1)}), bf16[1152,1024]{1,0:T(8,128)(2,1)}) %all-gather.8.cloned.1.call-update) | async-done | bytes 2359312 | tf_op jit(solution)/shard_map/all_gather | solution.py:76
  153.6 4.1 fusion.3
  157.7 0.8 copy-done.18
  158.7 2.4 convolution_bitcast_fusion.4
  161.2 27.2 %reduce-scatter.13.cloned.1.call-done = f32[64,1024]{1,0:T(8,128)} async-done(((f32[256,1024]{1,0:T(8,128)}), f32[64,1024]{1,0:T(8,128)}) %reduce-scatter.13.cloned.1.call-update) | async-done | bytes 262160 | tf_op jit(solution)/shard_map/reduce_scatter | solution.py:129
  188.4 1.2 multiply_reduce_fusion
  190.1 1.1 fusion.32
  191.3 15.9 %all_gather.35 = bf16[256,1024]{1,0:T(8,128)(2,1)S(1)} all-gather(bf16[64,1024]{1,0:T(8,128)(2,1)S(1)} %fusion.32), channel_id=1, replica_groups=mesh['dp'=8,'tensor'=4] {'tensor'}, dimensions={0}, use_global_device_ids=true | all-gather | bytes 655360 | tf_op jit(solution)/shard_map/all_gather | solution.py:132
  207.7 1.4 collective-permute-start.1
  209.1 1.7 collective-permute-done.1
  210.9 0.8 multiply_reduce_fusion.3
  211.8 1.4 fusion
  213.4 3.4 convolution_convert_fusion
  216.9 2.3 convolution_bitcast_fusion.2
  219.2 1.0 copy-done.3
  220.4 6.2 %convolution_bitcast_fusion = f32[2,1024,1152]{1,2,0:T(8,128)} fusion(bf16[1,256,1152]{2,1,0:T(8,128)(2,1)} %copy-done.20, bf16[1,256,1152]{2,1,0:T(8,128)(2,1)S(1)} %copy-done.19, bf16[256,1024]{1,0:T(8,128)(2,1)S(1)} %copy-done.3), kind=kOutput, calls=%fused_computation | convolution fusion | flops 1208549376 | bytes 11141120 | tf_op jit(solution)/shard_map/td,ktf->kdf/dot_general | solution.py:123
  226.6 0.8 copy-done.16
  227.4 1.3 fusion.39
  228.8 3.0 fusion.40
  232.6 1.5 reduce-scatter.15.cloned.1.call-done
  234.1 1.1 fusion.17
  235.2 39.3 %all-reduce = (f32[1024]{0:T(1024)}, f32[3,1024]{1,0:T(4,128)}, f32[1024]{0:T(1024)}) all-reduce(f32[1024]{0:T(1024)S(1)} %get-tuple-element.32, f32[3,1024]{1,0:T(4,128)S(1)} %maximum_dynamic-update-slice_fusion, f32[1024]{0:T(1024)S(1)} %get-tuple-element.30), channel_id=1, replica_groups=mesh['dp'=8,'tensor'=4] {'dp','tensor'}, use_global_device_ids=true, to_apply=%region_11.12 | all-reduce | flops 5120 | bytes 40960 | tf_op jit(solution)/shard_map/psum | solution.py:177
  274.6 1.9 fusion.14
  276.5 27.7 %reduce-scatter.17.cloned.1.call-done = f32[3,128,256]{1,2,0:T(8,128)} async-done(((f32[3,1024,256]{1,2,0:T(8,128)}), f32[3,128,256]{1,2,0:T(8,128)}) %reduce-scatter.17.cloned.1.call-update) | async-done | bytes 393232 | tf_op jit(solution)/shard_map/reduce_scatter | solution.py:172
  304.2 1.9 copy.25
  306.1 78.5 %reduce-scatter.21.cloned.1.call-done = f32[2,128,1152]{1,2,0:T(8,128)} async-done(((f32[2,1024,1152]{1,2,0:T(8,128)}), f32[2,128,1152]{1,2,0:T(8,128)}) %reduce-scatter.21.cloned.1.call-update) | async-done | bytes 1179664 | tf_op jit(solution)/shard_map/reduce_scatter | solution.py:174
  384.6 2.7 copy.26
  387.3 37.3 %reduce-scatter.19.cloned.1.call-done = f32[256,128]{1,0:T(8,128)} async-done(((f32[256,1024]{1,0:T(8,128)}), f32[256,128]{1,0:T(8,128)}) %reduce-scatter.19.cloned.1.call-update) | async-done | bytes 131088 | tf_op jit(solution)/shard_map/reduce_scatter | solution.py:173
  424.6 58.3 %reduce-scatter.23.cloned.1.call-done = f32[1152,128]{1,0:T(8,128)} async-done(((f32[1152,1024]{1,0:T(8,128)}), f32[1152,128]{1,0:T(8,128)}) %reduce-scatter.23.cloned.1.call-update) | async-done | bytes 589840 | tf_op jit(solution)/shard_map/reduce_scatter | solution.py:175
  (136 shorter events, 3.6 us)
Async XLA Ops:
  7.2 32.7 %all-gather.4.cloned.1.call-start = ((), (), s32[]{:S(2)}) async-start(), calls=%async_computation.8 | async-start | bytes 1769472 | tf_op jit(solution)/shard_map/all_gather | solution.py:73
  7.9 74.5 %reduce-scatter.9.cloned.1.call-start = ((), (), s32[]{:S(2)}) async-start(), calls=%async_computation.9 | async-start | bytes 1310720 | tf_op jit(solution)/shard_map/reduce_scatter | solution.py:92
  20.6 24.5 %copy-start.4 = (bf16[256,1024]{1,0:T(8,128)(2,1)}, bf16[256,1024]{1,0:T(8,128)(2,1)S(1)}, u32[]{:S(2)}) copy-start(bf16[256,1024]{1,0:T(8,128)(2,1)S(1)} %all_gather.30) | copy-start | bytes 1572868
  21.8 17.5 %copy-start.40 = (f32[64]{0:T(128)}, f32[64]{0:T(128)S(1)}, u32[]{:S(2)}) copy-start(f32[64]{0:T(128)S(1)} %add_rsqrt_fusion.1) | copy-start | bytes 772
  39.2 2.8 copy-start.6
  39.9 4.3 copy-start.33
  39.9 4.3 copy-start.35
  42.0 2.2 collective-permute-start
  45.1 2.1 copy-start.15
  45.1 2.7 copy-start.13
  46.4 36.0 %copy-start.8 = (bf16[64,1024]{1,0:T(8,128)(2,1)S(1)}, bf16[64,1024]{1,0:T(8,128)(2,1)}, u32[]{:S(2)}) copy-start(bf16[64,1024]{1,0:T(8,128)(2,1)} %param.10) | copy-start | bytes 393220
  46.4 37.1 %copy-start.25 = (f32[1024]{0:T(1024)S(1)}, f32[1024]{0:T(1024)}, u32[]{:S(2)}) copy-start(f32[1024]{0:T(1024)} %param.15) | copy-start | bytes 12292
  46.4 75.9 %all-gather.6.cloned.1.call-start = ((), (), s32[]{:S(2)}) async-start(), calls=%async_computation.10 | async-start | bytes 5308416 | tf_op jit(solution)/shard_map/all_gather | solution.py:75
  47.2 106.4 %all-gather.8.cloned.1.call-start = ((), (), s32[]{:S(2)}) async-start(), calls=%async_computation.11 | async-start | bytes 2654208 | tf_op jit(solution)/shard_map/all_gather | solution.py:76
  47.8 140.6 %reduce-scatter.13.cloned.1.call-start = ((), (), s32[]{:S(2)}) async-start(), calls=%async_computation.13 | async-start | bytes 1310720 | tf_op jit(solution)/shard_map/reduce_scatter | solution.py:129
  83.5 16.8 %copy-start.1 = (f32[64,1024]{1,0:T(8,128)}, f32[64,1024]{1,0:T(8,128)S(1)}, u32[]{:S(2)}) copy-start(f32[64,1024]{1,0:T(8,128)S(1)} %get-tuple-element.40) | copy-start | bytes 786436
  83.5 16.8 %copy-start.37 = (f32[64]{0:T(128)}, f32[64]{0:T(128)S(1)}, u32[]{:S(2)}) copy-start(f32[64]{0:T(128)S(1)} %add_rsqrt_fusion) | copy-start | bytes 772
  153.6 5.1 %copy-start = (bf16[2,1024,1152]{2,1,0:T(8,128)(2,1)S(1)}, bf16[2,1024,1152]{2,1,0:T(8,128)(2,1)}, u32[]{:S(2)}) copy-start(bf16[2,1024,1152]{2,1,0:T(8,128)(2,1)} %all-gather.6.cloned.1.call-done) | copy-start | bytes 14155780
  158.7 29.7 %copy-start.2 = (f32[64,1024]{1,0:T(8,128)S(1)}, f32[64,1024]{1,0:T(8,128)}, u32[]{:S(2)}) copy-start(f32[64,1024]{1,0:T(8,128)} %copy-done.1) | copy-start | bytes 786436
  158.7 29.7 %copy-start.38 = (f32[64]{0:T(128)S(1)}, f32[64]{0:T(128)}, u32[]{:S(2)}) copy-start(f32[64]{0:T(128)} %copy-done.37) | copy-start | bytes 772
  161.1 29.0 %copy-start.14 = (bf16[64,1024]{1,0:T(8,128)(2,1)S(1)}, bf16[64,1024]{1,0:T(8,128)(2,1)}, u32[]{:S(2)}) copy-start(bf16[64,1024]{1,0:T(8,128)(2,1)} %param.18) | copy-start | bytes 393220
  161.1 46.1 %copy-start.5 = (bf16[256,1024]{1,0:T(8,128)(2,1)S(1)}, bf16[256,1024]{1,0:T(8,128)(2,1)}, u32[]{:S(2)}) copy-start(bf16[256,1024]{1,0:T(8,128)(2,1)} %copy-done.4) | copy-start | bytes 1572868
  161.1 46.4 %copy-start.17 = (f32[256,256]{1,0:T(8,128)S(1)}, f32[256,256]{1,0:T(8,128)}, u32[]{:S(2)}) copy-start(f32[256,256]{1,0:T(8,128)} %get-tuple-element.42) | copy-start | bytes 786436
  161.1 73.0 %reduce-scatter.15.cloned.1.call-start = ((), (), s32[]{:S(2)}) async-start(), calls=%async_computation.14 | async-start | bytes 655360 | tf_op jit(solution)/shard_map/reduce_scatter | solution.py:166
  191.2 19.6 %copy-start.28 = (f32[1,256]{1,0:T(1,128)S(1)}, f32[1,256]{1,0:T(1,128)}, u32[]{:S(2)}) copy-start(f32[1,256]{1,0:T(1,128)} %copy-done.27) | copy-start | bytes 3076
  191.2 19.6 %copy-start.30 = (f32[1,256]{1,0:T(1,128)S(1)}, f32[1,256]{1,0:T(1,128)}, u32[]{:S(2)}) copy-start(f32[1,256]{1,0:T(1,128)} %copy-done.29) | copy-start | bytes 3076
  191.2 19.6 %copy-start.32 = (f32[1,256]{1,0:T(1,128)S(1)}, f32[1,256]{1,0:T(1,128)}, u32[]{:S(2)}) copy-start(f32[1,256]{1,0:T(1,128)} %copy-done.31) | copy-start | bytes 3076
  191.2 19.6 %copy-start.34 = (f32[256]{0:T(256)S(1)}, f32[256]{0:T(256)}, u32[]{:S(2)}) copy-start(f32[256]{0:T(256)} %copy-done.33) | copy-start | bytes 3076
  191.2 19.6 %copy-start.36 = (f32[256]{0:T(256)S(1)}, f32[256]{0:T(256)}, u32[]{:S(2)}) copy-start(f32[256]{0:T(256)} %copy-done.35) | copy-start | bytes 3076
  191.3 19.6 %copy-start.45 = (f32[256]{0:T(256)S(1)}, f32[256]{0:T(256)}, u32[]{:S(2)}) copy-start(f32[256]{0:T(256)} %get-tuple-element.57) | copy-start | bytes 3076
  191.3 19.6 %copy-start.46 = (f32[256]{0:T(256)S(1)}, f32[256]{0:T(256)}, u32[]{:S(2)}) copy-start(f32[256]{0:T(256)} %get-tuple-element.62) | copy-start | bytes 3076
  207.6 4.2 copy-start.23
  207.7 4.2 copy-start.11
  207.7 3.2 collective-permute-start.1
  213.3 61.3 %reduce-scatter.11.cloned.1.call-start = ((), (), s32[]{:S(2)}) async-start(), calls=%async_computation.12 | async-start | bytes 655360 | tf_op jit(solution)/shard_map/reduce_scatter | solution.py:105
  213.3 3.5 copy-start.7
  213.3 3.5 copy-start.22
  213.4 3.5 copy-start.24
  216.8 87.4 %reduce-scatter.17.cloned.1.call-start = ((), (), s32[]{:S(2)}) async-start(), calls=%async_computation.15 | async-start | bytes 3538944 | tf_op jit(solution)/shard_map/reduce_scatter | solution.py:172
  219.2 165.5 %reduce-scatter.21.cloned.1.call-start = ((), (), s32[]{:S(2)}) async-start(), calls=%async_computation.17 | async-start | bytes 10616832 | tf_op jit(solution)/shard_map/reduce_scatter | solution.py:174
  226.6 2.3 copy-start.10
  226.6 198.1 %reduce-scatter.19.cloned.1.call-start = ((), (), s32[]{:S(2)}) async-start(), calls=%async_computation.16 | async-start | bytes 1179648 | tf_op jit(solution)/shard_map/reduce_scatter | solution.py:173
  228.8 254.2 %reduce-scatter.23.cloned.1.call-start = ((), (), s32[]{:S(2)}) async-start(), calls=%async_computation.18 | async-start | bytes 5308416 | tf_op jit(solution)/shard_map/reduce_scatter | solution.py:175
  231.9 2.2 copy-start.26
  231.9 2.2 copy-start.41
  231.9 42.7 %copy-start.9 = (f32[64,1024]{1,0:T(8,128)S(1)}, f32[64,1024]{1,0:T(8,128)}, u32[]{:S(2)}) copy-start(f32[64,1024]{1,0:T(8,128)} %reduce-scatter.13.cloned.1.call-done) | copy-start | bytes 786436
  231.9 42.7 %copy-start.39 = (f32[64]{0:T(128)S(1)}, f32[64]{0:T(128)}, u32[]{:S(2)}) copy-start(f32[64]{0:T(128)} %copy-done.37) | copy-start | bytes 772
  231.9 42.7 %copy-start.48 = (f32[64]{0:T(128)S(1)}, f32[64]{0:T(128)}, u32[]{:S(2)}) copy-start(f32[64]{0:T(128)} %copy-done.47) | copy-start | bytes 772
  (14 other events, 13.4 us)
Sparse Core Ops, SparseCore 0:
  9.9 28.3 all-gather.3
  46.6 35.7 reduce-scatter.8
  84.4 37.8 all-gather.5
  124.2 29.3 all-gather.7
  161.2 27.1 reduce-scatter.12
  213.4 20.6 reduce-scatter.14
  236.4 19.9 reduce-scatter.10
  259.8 44.4 reduce-scatter.16
  308.1 76.4 reduce-scatter.20
  388.6 36.0 reduce-scatter.18
  429.0 53.8 reduce-scatter.22
where the time goes:
time: 490 us; the launch traced here: 489 us
  waiting for transfers between devices  297 us (61%)
  blocking collectives  121 us (25%)
  matrix products  31.5 us (6%)
  between operations  14.5 us (3%)
  other arithmetic  11.5 us (2%)
  local copies, waits for them, and re-layouts  10.4 us (2%)
    reduce_scatter x1, waiting for transfers between devices, shards(): lax.psum_scatter(gate_up_part, 'dp', scatter_dimension=1, tiled=True)  78.5 us
    reduce_scatter x1, waiting for transfers between devices, shards(): lax.psum_scatter(down_part, 'dp', scatter_dimension=1, tiled=True)  58.3 us
    psum x1, blocking collectives, shards(): lax.psum((first_part, second_part, kernel_full), ('dp', 'tensor'))  39.3 us
    reduce_scatter x1, waiting for transfers between devices, shards(): lax.psum_scatter(out_part, 'dp', scatter_dimension=1, tiled=True)  37.3 us
    reduce_scatter x1, waiting for transfers between devices, shards(): lax.psum_scatter(in_part, 'dp', scatter_dimension=1, tiled=True)  27.7 us
    all_gather x1, waiting for transfers between devices, shards(): lax.all_gather(down_weight, 'dp', axis=1, tiled=True)  27.4 us
    reduce_scatter x1, waiting for transfers between devices, shards(): lax.psum_scatter(hidden_back, 'tensor', scatter_dimension=0, tiled=True)  27.2 us
    all_gather x1, waiting for transfers between devices, shards(): lax.all_gather(gate_up_weight, 'dp', axis=1, tiled=True)  22.1 us
  transfers between devices with their start and end apart: 13, of which 10 were waited for; matrix products, arithmetic and copies ran while one was open for 7% of the time, Pallas kernels for 0%

commit v1 on v0

--- a/solution.py
+++ b/solution.py
@@ -1,9 +1,19 @@
+import functools
 import jax
 import jax.numpy as jnp
 from jax import lax
 from jax.sharding import PartitionSpec as P
 
 EPS = 1e-05
+
+
+def proceed_teams_over_axis(unit, mesh_ax, net_axis):
+    for i0 in (mesh_ax, net_axis):
+        unit = lax.psum(unit, i0)
+    return unit
+
+
+perform_tiles_on = functools.partial(proceed_teams_over_axis, mesh_ax="tensor", net_axis="dp")
 
 
 def passed_along(block, axis, distance):
@@ -174,8 +184,8 @@
         lax.psum_scatter(gate_up_part, "dp", scatter_dimension=1, tiled=True),
         lax.psum_scatter(down_part, "dp", scatter_dimension=1, tiled=True),
     )
-    first_gain_grad, second_gain_grad, conv_grad = lax.psum(
-        (first_part, second_part, kernel_full), ("dp", "tensor")
+    first_gain_grad, second_gain_grad, conv_grad = perform_tiles_on(
+        (first_part, second_part, kernel_full)
     )
     return (
         output,

time: 490 us -> 490 us (level)
    psum x1 -> x2, blocking collectives: 39.3 us -> 39.5 us  [proceed_teams_over_axis(): unit = lax.psum(unit, i0)]
where the time goes in v1:
time: 490 us; the launch traced here: 489 us
  waiting for transfers between devices  297 us (61%)
  blocking collectives  122 us (25%)
  matrix products  31.5 us (6%)
  between operations  14.5 us (3%)
  other arithmetic  11.5 us (2%)
  local copies, waits for them, and re-layouts  10.4 us (2%)
    reduce_scatter x1, waiting for transfers between devices, shards(): lax.psum_scatter(gate_up_part, 'dp', scatter_dimension=1, tiled=True)  78.5 us
    reduce_scatter x1, waiting for transfers between devices, shards(): lax.psum_scatter(down_part, 'dp', scatter_dimension=1, tiled=True)  58.3 us
    psum x2, blocking collectives, proceed_teams_over_axis(): unit = lax.psum(unit, i0)  39.5 us
    reduce_scatter x1, waiting for transfers between devices, shards(): lax.psum_scatter(out_part, 'dp', scatter_dimension=1, tiled=True)  37.3 us
    reduce_scatter x1, waiting for transfers between devices, shards(): lax.psum_scatter(in_part, 'dp', scatter_dimension=1, tiled=True)  27.4 us
    all_gather x1, waiting for transfers between devices, shards(): lax.all_gather(down_weight, 'dp', axis=1, tiled=True)  27.4 us
    reduce_scatter x1, waiting for transfers between devices, shards(): lax.psum_scatter(hidden_back, 'tensor', scatter_dimension=0, tiled=True)  27.2 us
    all_gather x1, waiting for transfers between devices, shards(): lax.all_gather(gate_up_weight, 'dp', axis=1, tiled=True)  22.1 us
  transfers between devices with their start and end apart: 13, of which 10 were waited for; matrix products, arithmetic and copies ran while one was open for 7% of the time, Pallas kernels for 0%

profile of v1, /device:TPU:0, one launch (start us, length us, event | category | flops | bytes accessed | tf_op | source)
XLA Modules:
  0.0 489.5 jit_solution(7870595740377648362)
XLA Ops:
  7.2 0.7 all-gather.4.cloned.1.call-update
  8.0 0.8 reduce-window.8
  8.9 11.7 %all_gather.30 = bf16[256,1024]{1,0:T(8,128)(2,1)S(1)} all-gather(bf16[256,128]{1,0:T(8,128)(2,1)} %param.14), channel_id=1, replica_groups=mesh['dp'=8,'tensor'=4] {'dp'}, dimensions={1}, use_global_device_ids=true | all-gather | bytes 589824 | tf_op jit(solution)/shard_map/all_gather | solution.py:84
  20.6 1.1 fusion.18
  21.8 1.0 fusion.15
  22.8 16.4 %all_gather.28 = bf16[256,1024]{1,0:T(8,128)(2,1)S(1)} all-gather(bf16[64,1024]{1,0:T(8,128)(2,1)S(1)} %fusion.15), channel_id=1, replica_groups=mesh['dp'=8,'tensor'=4] {'tensor'}, dimensions={0}, use_global_device_ids=true | all-gather | bytes 655360 | tf_op jit(solution)/shard_map/all_gather | solution.py:79
  39.9 2.0 convolution_bitcast_fusion.5
  42.0 1.3 collective-permute-start
  43.3 0.9 fusion.34
  44.2 0.9 multiply_convert_fusion.8
  45.1 1.3 fusion.37
  46.5 0.7 all-gather.6.cloned.1.call-update
  47.8 21.5 %all_gather.34 = bf16[256,1024]{1,0:T(8,128)(2,1)} all-gather(bf16[64,1024]{1,0:T(8,128)(2,1)S(1)} %copy-done.13), channel_id=1, replica_groups=mesh['dp'=8,'tensor'=4] {'tensor'}, dimensions={0}, use_global_device_ids=true | all-gather | bytes 655360 | tf_op jit(solution)/shard_map/all_gather | solution.py:125
  69.3 13.1 %reduce-scatter.9.cloned.1.call-done = f32[64,1024]{1,0:T(8,128)} async-done(((f32[256,1024]{1,0:T(8,128)}), f32[64,1024]{1,0:T(8,128)}) %reduce-scatter.9.cloned.1.call-update) | async-done | bytes 262160 | tf_op jit(solution)/shard_map/reduce_scatter | solution.py:102
  82.4 1.1 multiply_reduce_fusion.5
  83.6 16.7 %all_gather.31 = bf16[256,1024]{1,0:T(8,128)(2,1)} all-gather(bf16[64,1024]{1,0:T(8,128)(2,1)S(1)} %multiply_convert_fusion.7), channel_id=1, replica_groups=mesh['dp'=8,'tensor'=4] {'tensor'}, dimensions={0}, use_global_device_ids=true | all-gather | bytes 655360 | tf_op jit(solution)/shard_map/all_gather | solution.py:103
  100.3 22.1 %all-gather.6.cloned.1.call-done = bf16[2,1024,1152]{2,1,0:T(8,128)(2,1)} async-done(((bf16[2,128,1152]{2,1,0:T(8,128)(2,1)}), bf16[2,1024,1152]{2,1,0:T(8,128)(2,1)}) %all-gather.6.cloned.1.call-update) | async-done | bytes 4718608 | tf_op jit(solution)/shard_map/all_gather | solution.py:85
  122.4 3.9 convolution_bitcast_fusion.1
  126.2 27.4 %all-gather.8.cloned.1.call-done = bf16[1152,1024]{1,0:T(8,128)(2,1)} async-done(((bf16[1152,128]{1,0:T(8,128)(2,1)}), bf16[1152,1024]{1,0:T(8,128)(2,1)}) %all-gather.8.cloned.1.call-update) | async-done | bytes 2359312 | tf_op jit(solution)/shard_map/all_gather | solution.py:86
  153.6 4.1 fusion.3
  157.7 0.8 copy-done.18
  158.7 2.4 convolution_bitcast_fusion.4
  161.2 27.2 %reduce-scatter.13.cloned.1.call-done = f32[64,1024]{1,0:T(8,128)} async-done(((f32[256,1024]{1,0:T(8,128)}), f32[64,1024]{1,0:T(8,128)}) %reduce-scatter.13.cloned.1.call-update) | async-done | bytes 262160 | tf_op jit(solution)/shard_map/reduce_scatter | solution.py:139
  188.4 1.2 multiply_reduce_fusion
  190.1 1.1 fusion.32
  191.3 15.9 %all_gather.35 = bf16[256,1024]{1,0:T(8,128)(2,1)S(1)} all-gather(bf16[64,1024]{1,0:T(8,128)(2,1)S(1)} %fusion.32), channel_id=1, replica_groups=mesh['dp'=8,'tensor'=4] {'tensor'}, dimensions={0}, use_global_device_ids=true | all-gather | bytes 655360 | tf_op jit(solution)/shard_map/all_gather | solution.py:142
  207.7 1.4 collective-permute-start.1
  209.1 1.7 collective-permute-done.1
  210.9 0.8 multiply_reduce_fusion.3
  211.8 1.4 fusion
  213.4 3.4 convolution_convert_fusion
  216.9 2.3 convolution_bitcast_fusion.2
  219.2 1.0 copy-done.3
  220.4 6.1 %convolution_bitcast_fusion = f32[2,1024,1152]{1,2,0:T(8,128)} fusion(bf16[1,256,1152]{2,1,0:T(8,128)(2,1)} %copy-done.20, bf16[1,256,1152]{2,1,0:T(8,128)(2,1)S(1)} %copy-done.19, bf16[256,1024]{1,0:T(8,128)(2,1)S(1)} %copy-done.3), kind=kOutput, calls=%fused_computation | convolution fusion | flops 1208549376 | bytes 11141120 | tf_op jit(solution)/shard_map/td,ktf->kdf/dot_general | solution.py:133
  226.6 0.8 copy-done.16
  227.4 1.3 fusion.39
  228.8 3.0 fusion.40
  232.6 1.5 reduce-scatter.15.cloned.1.call-done
  234.1 1.1 fusion.17
  235.3 16.2 %all-reduce.1 = (f32[1024]{0:T(1024)S(1)}, f32[3,1024]{1,0:T(4,128)S(1)}, f32[1024]{0:T(1024)S(1)}) all-reduce(f32[1024]{0:T(1024)S(1)} %get-tuple-element.32, f32[3,1024]{1,0:T(4,128)S(1)} %maximum_dynamic-update-slice_fusion, f32[1024]{0:T(1024)S(1)} %get-tuple-element.30), channel_id=1, replica_groups=mesh['dp'=8,'tensor'=4] {'tensor'}, use_global_device_ids=true, to_apply=%region_11.12 | all-reduce | flops 5120 | bytes 40960 | tf_op jit(solution)/shard_map/psum | solution.py:12
  251.4 23.4 %all-reduce = (f32[1024]{0:T(1024)}, f32[3,1024]{1,0:T(4,128)}, f32[1024]{0:T(1024)}) all-reduce(f32[1024]{0:T(1024)S(1)} %get-tuple-element.37, f32[3,1024]{1,0:T(4,128)S(1)} %get-tuple-element.38, f32[1024]{0:T(1024)S(1)} %get-tuple-element.39), channel_id=1, replica_groups=mesh['dp'=8,'tensor'=4] {'dp'}, use_global_device_ids=true, to_apply=%region_12.13 | all-reduce | flops 5120 | bytes 40960 | tf_op jit(solution)/shard_map/psum | solution.py:12
  274.8 1.9 fusion.14
  276.7 27.4 %reduce-scatter.17.cloned.1.call-done = f32[3,128,256]{1,2,0:T(8,128)} async-done(((f32[3,1024,256]{1,2,0:T(8,128)}), f32[3,128,256]{1,2,0:T(8,128)}) %reduce-scatter.17.cloned.1.call-update) | async-done | bytes 393232 | tf_op jit(solution)/shard_map/reduce_scatter | solution.py:182
  304.2 1.9 copy.25
  306.1 78.5 %reduce-scatter.21.cloned.1.call-done = f32[2,128,1152]{1,2,0:T(8,128)} async-done(((f32[2,1024,1152]{1,2,0:T(8,128)}), f32[2,128,1152]{1,2,0:T(8,128)}) %reduce-scatter.21.cloned.1.call-update) | async-done | bytes 1179664 | tf_op jit(solution)/shard_map/reduce_scatter | solution.py:184
  384.6 2.7 copy.26
  387.3 37.3 %reduce-scatter.19.cloned.1.call-done = f32[256,128]{1,0:T(8,128)} async-done(((f32[256,1024]{1,0:T(8,128)}), f32[256,128]{1,0:T(8,128)}) %reduce-scatter.19.cloned.1.call-update) | async-done | bytes 131088 | tf_op jit(solution)/shard_map/reduce_scatter | solution.py:183
  424.6 58.3 %reduce-scatter.23.cloned.1.call-done = f32[1152,128]{1,0:T(8,128)} async-done(((f32[1152,1024]{1,0:T(8,128)}), f32[1152,128]{1,0:T(8,128)}) %reduce-scatter.23.cloned.1.call-update) | async-done | bytes 589840 | tf_op jit(solution)/shard_map/reduce_scatter | solution.py:185
  (137 shorter events, 4.2 us)
Async XLA Ops:
  7.2 32.7 %all-gather.4.cloned.1.call-start = ((), (), s32[]{:S(2)}) async-start(), calls=%async_computation.8 | async-start | bytes 1769472 | tf_op jit(solution)/shard_map/all_gather | solution.py:83
  7.9 74.5 %reduce-scatter.9.cloned.1.call-start = ((), (), s32[]{:S(2)}) async-start(), calls=%async_computation.9 | async-start | bytes 1310720 | tf_op jit(solution)/shard_map/reduce_scatter | solution.py:102
  20.6 24.5 %copy-start.4 = (bf16[256,1024]{1,0:T(8,128)(2,1)}, bf16[256,1024]{1,0:T(8,128)(2,1)S(1)}, u32[]{:S(2)}) copy-start(bf16[256,1024]{1,0:T(8,128)(2,1)S(1)} %all_gather.30) | copy-start | bytes 1572868
  21.8 17.5 %copy-start.40 = (f32[64]{0:T(128)}, f32[64]{0:T(128)S(1)}, u32[]{:S(2)}) copy-start(f32[64]{0:T(128)S(1)} %add_rsqrt_fusion.1) | copy-start | bytes 772
  39.2 2.8 copy-start.6
  39.9 4.3 copy-start.33
  39.9 4.3 copy-start.35
  42.0 2.2 collective-permute-start
  45.1 2.1 copy-start.15
  45.1 2.7 copy-start.13
  46.4 36.0 %copy-start.8 = (bf16[64,1024]{1,0:T(8,128)(2,1)S(1)}, bf16[64,1024]{1,0:T(8,128)(2,1)}, u32[]{:S(2)}) copy-start(bf16[64,1024]{1,0:T(8,128)(2,1)} %param.10) | copy-start | bytes 393220
  46.4 37.1 %copy-start.25 = (f32[1024]{0:T(1024)S(1)}, f32[1024]{0:T(1024)}, u32[]{:S(2)}) copy-start(f32[1024]{0:T(1024)} %param.15) | copy-start | bytes 12292
  46.4 75.9 %all-gather.6.cloned.1.call-start = ((), (), s32[]{:S(2)}) async-start(), calls=%async_computation.10 | async-start | bytes 5308416 | tf_op jit(solution)/shard_map/all_gather | solution.py:85
  47.2 106.4 %all-gather.8.cloned.1.call-start = ((), (), s32[]{:S(2)}) async-start(), calls=%async_computation.11 | async-start | bytes 2654208 | tf_op jit(solution)/shard_map/all_gather | solution.py:86
  47.8 140.6 %reduce-scatter.13.cloned.1.call-start = ((), (), s32[]{:S(2)}) async-start(), calls=%async_computation.13 | async-start | bytes 1310720 | tf_op jit(solution)/shard_map/reduce_scatter | solution.py:139
  83.5 16.8 %copy-start.1 = (f32[64,1024]{1,0:T(8,128)}, f32[64,1024]{1,0:T(8,128)S(1)}, u32[]{:S(2)}) copy-start(f32[64,1024]{1,0:T(8,128)S(1)} %get-tuple-element.43) | copy-start | bytes 786436
  83.5 16.8 %copy-start.37 = (f32[64]{0:T(128)}, f32[64]{0:T(128)S(1)}, u32[]{:S(2)}) copy-start(f32[64]{0:T(128)S(1)} %add_rsqrt_fusion) | copy-start | bytes 772
  153.6 5.1 %copy-start = (bf16[2,1024,1152]{2,1,0:T(8,128)(2,1)S(1)}, bf16[2,1024,1152]{2,1,0:T(8,128)(2,1)}, u32[]{:S(2)}) copy-start(bf16[2,1024,1152]{2,1,0:T(8,128)(2,1)} %all-gather.6.cloned.1.call-done) | copy-start | bytes 14155780
  158.7 29.7 %copy-start.2 = (f32[64,1024]{1,0:T(8,128)S(1)}, f32[64,1024]{1,0:T(8,128)}, u32[]{:S(2)}) copy-start(f32[64,1024]{1,0:T(8,128)} %copy-done.1) | copy-start | bytes 786436
  158.7 29.7 %copy-start.38 = (f32[64]{0:T(128)S(1)}, f32[64]{0:T(128)}, u32[]{:S(2)}) copy-start(f32[64]{0:T(128)} %copy-done.37) | copy-start | bytes 772
  161.1 29.0 %copy-start.14 = (bf16[64,1024]{1,0:T(8,128)(2,1)S(1)}, bf16[64,1024]{1,0:T(8,128)(2,1)}, u32[]{:S(2)}) copy-start(bf16[64,1024]{1,0:T(8,128)(2,1)} %param.18) | copy-start | bytes 393220
  161.1 46.1 %copy-start.5 = (bf16[256,1024]{1,0:T(8,128)(2,1)S(1)}, bf16[256,1024]{1,0:T(8,128)(2,1)}, u32[]{:S(2)}) copy-start(bf16[256,1024]{1,0:T(8,128)(2,1)} %copy-done.4) | copy-start | bytes 1572868
  161.1 46.4 %copy-start.17 = (f32[256,256]{1,0:T(8,128)S(1)}, f32[256,256]{1,0:T(8,128)}, u32[]{:S(2)}) copy-start(f32[256,256]{1,0:T(8,128)} %get-tuple-element.45) | copy-start | bytes 786436
  161.1 73.0 %reduce-scatter.15.cloned.1.call-start = ((), (), s32[]{:S(2)}) async-start(), calls=%async_computation.14 | async-start | bytes 655360 | tf_op jit(solution)/shard_map/reduce_scatter | solution.py:176
  191.2 19.7 %copy-start.28 = (f32[1,256]{1,0:T(1,128)S(1)}, f32[1,256]{1,0:T(1,128)}, u32[]{:S(2)}) copy-start(f32[1,256]{1,0:T(1,128)} %copy-done.27) | copy-start | bytes 3076
  191.2 19.7 %copy-start.30 = (f32[1,256]{1,0:T(1,128)S(1)}, f32[1,256]{1,0:T(1,128)}, u32[]{:S(2)}) copy-start(f32[1,256]{1,0:T(1,128)} %copy-done.29) | copy-start | bytes 3076
  191.2 19.7 %copy-start.32 = (f32[1,256]{1,0:T(1,128)S(1)}, f32[1,256]{1,0:T(1,128)}, u32[]{:S(2)}) copy-start(f32[1,256]{1,0:T(1,128)} %copy-done.31) | copy-start | bytes 3076
  191.2 19.7 %copy-start.34 = (f32[256]{0:T(256)S(1)}, f32[256]{0:T(256)}, u32[]{:S(2)}) copy-start(f32[256]{0:T(256)} %copy-done.33) | copy-start | bytes 3076
  191.2 19.6 %copy-start.36 = (f32[256]{0:T(256)S(1)}, f32[256]{0:T(256)}, u32[]{:S(2)}) copy-start(f32[256]{0:T(256)} %copy-done.35) | copy-start | bytes 3076
  191.3 19.6 %copy-start.45 = (f32[256]{0:T(256)S(1)}, f32[256]{0:T(256)}, u32[]{:S(2)}) copy-start(f32[256]{0:T(256)} %get-tuple-element.60) | copy-start | bytes 3076
  191.3 19.6 %copy-start.46 = (f32[256]{0:T(256)S(1)}, f32[256]{0:T(256)}, u32[]{:S(2)}) copy-start(f32[256]{0:T(256)} %get-tuple-element.65) | copy-start | bytes 3076
  207.6 4.2 copy-start.23
  207.7 4.2 copy-start.11
  207.7 3.2 collective-permute-start.1
  213.3 61.5 %reduce-scatter.11.cloned.1.call-start = ((), (), s32[]{:S(2)}) async-start(), calls=%async_computation.12 | async-start | bytes 655360 | tf_op jit(solution)/shard_map/reduce_scatter | solution.py:115
  213.3 3.5 copy-start.7
  213.3 3.5 copy-start.22
  213.4 3.5 copy-start.24
  216.8 87.3 %reduce-scatter.17.cloned.1.call-start = ((), (), s32[]{:S(2)}) async-start(), calls=%async_computation.15 | async-start | bytes 3538944 | tf_op jit(solution)/shard_map/reduce_scatter | solution.py:182
  219.2 165.4 %reduce-scatter.21.cloned.1.call-start = ((), (), s32[]{:S(2)}) async-start(), calls=%async_computation.17 | async-start | bytes 10616832 | tf_op jit(solution)/shard_map/reduce_scatter | solution.py:184
  226.6 2.3 copy-start.10
  226.6 198.0 %reduce-scatter.19.cloned.1.call-start = ((), (), s32[]{:S(2)}) async-start(), calls=%async_computation.16 | async-start | bytes 1179648 | tf_op jit(solution)/shard_map/reduce_scatter | solution.py:183
  228.8 254.2 %reduce-scatter.23.cloned.1.call-start = ((), (), s32[]{:S(2)}) async-start(), calls=%async_computation.18 | async-start | bytes 5308416 | tf_op jit(solution)/shard_map/reduce_scatter | solution.py:185
  231.9 2.3 copy-start.26
  231.9 2.3 copy-start.41
  231.9 42.9 %copy-start.9 = (f32[64,1024]{1,0:T(8,128)S(1)}, f32[64,1024]{1,0:T(8,128)}, u32[]{:S(2)}) copy-start(f32[64,1024]{1,0:T(8,128)} %reduce-scatter.13.cloned.1.call-done) | copy-start | bytes 786436
  231.9 42.9 %copy-start.39 = (f32[64]{0:T(128)S(1)}, f32[64]{0:T(128)}, u32[]{:S(2)}) copy-start(f32[64]{0:T(128)} %copy-done.37) | copy-start | bytes 772
  231.9 42.9 %copy-start.48 = (f32[64]{0:T(128)S(1)}, f32[64]{0:T(128)}, u32[]{:S(2)}) copy-start(f32[64]{0:T(128)} %copy-done.47) | copy-start | bytes 772
  (14 other events, 13.4 us)
Sparse Core Ops, SparseCore 0:
  9.9 28.3 all-gather.3
  46.6 35.7 reduce-scatter.8
  84.4 37.8 all-gather.5
  124.2 29.3 all-gather.7
  161.2 27.1 reduce-scatter.12
  213.4 20.6 reduce-scatter.14
  236.4 19.9 reduce-scatter.10
  259.8 44.3 reduce-scatter.16
  308.1 76.4 reduce-scatter.20
  388.5 36.0 reduce-scatter.18
  429.0 53.8 reduce-scatter.22
